TPU v7x, 1024 devices: a whole 4x8x16 slice. The times are simulated.
1024 devices in a mesh: expert: 16 (over y, core), tensor: 16 (over z), dp: 4 (over x).
Axes of the slice: x: 4, y: 8, z: 16, core: 2. Of those that a mesh axis runs over, the one named last changes fastest.
Arguments:
- cotangent: bfloat16 [64, 128, 7168], P(('expert', 'dp'), 'tensor'), may hold values from -6 to 6
- routed_expert_index: int32 [64, 128, 8], P(('expert', 'dp')), may hold values from 0 to 127, all different within a row; in each aligned block of 128 rows (0 to 127, 128 to 255, ..., all dimensions but the last counted through in order) at most 12 rows name the same one
- chosen_gate_weight: float32 [64, 128, 8], P(('expert', 'dp')), may hold values from 0.05 to 0.6
- routed_down_weight: bfloat16 [128, 1024, 7168], P(('expert', 'dp'), None, 'tensor'), may hold values from -0.1875 to 0.1875
- routed_adapter_input_map: bfloat16 [128, 1024, 16], P(('expert', 'dp'), 'tensor'), may hold values from -0.1875 to 0.1875
- routed_adapter_output_map: bfloat16 [128, 16, 7168], P(('expert', 'dp'), None, 'tensor'), may hold values from -0.0625 to 0.0625
- routed_gate_saved: bfloat16 [1024, 128, 768], P('tensor', ('expert', 'dp')), may hold values from -6 to 6
- routed_up_saved: bfloat16 [1024, 128, 768], P('tensor', ('expert', 'dp')), may hold values from -6 to 6
- shared_down_weight: bfloat16 [2048, 7168], P('tensor'), may hold values from -0.125 to 0.125
- shared_adapter_input_map: bfloat16 [2048, 16], P('tensor'), may hold values from -0.125 to 0.125
- shared_adapter_output_map: bfloat16 [16, 7168], replicated, may hold values from -0.0625 to 0.0625
- shared_gate_saved: bfloat16 [64, 128, 2048], P(('expert', 'dp'), None, 'tensor'), may hold values from -6 to 6
- shared_up_saved: bfloat16 [64, 128, 2048], P(('expert', 'dp'), None, 'tensor'), may hold values from -6 to 6
Outputs:
- grad_gate_routed: bfloat16 [1024, 128, 768], P('tensor', ('expert', 'dp'))
- grad_up_routed: bfloat16 [1024, 128, 768], P('tensor', ('expert', 'dp'))
- grad_gate_shared: bfloat16 [64, 128, 2048], P(('expert', 'dp'), None, 'tensor')
- grad_up_shared: bfloat16 [64, 128, 2048], P(('expert', 'dp'), None, 'tensor')
- grad_a_routed: float32 [128, 1024, 16], P(('expert', 'dp'), 'tensor')
- grad_b_routed: float32 [128, 16, 7168], P(('expert', 'dp'), None, 'tensor')
- grad_a_shared: float32 [2048, 16], P('tensor')
- grad_b_shared: float32 [16, 7168], P(None, 'tensor')
Inputs may be any that keep to these rules, and one draw needn't show every extreme that they name: `routed_expert_index`: each token names 8 different experts; within one token group no expert is named by more than 12 tokens, and in some group one expert is named by exactly 12.
All inputs are finite; a program needn't handle non-finite values.
Results may differ from a plain program's by a relative error of at most 0.024.
Values may be sent and summed in bfloat16 or wider, within the bound.
No kernel may reach another device: no remote copies, remote signals or barrier semaphores. Data moves between devices by JAX's collectives and lax.ppermute only.
A program may use at most 64 MiB of HBM per device.

v0:
```python
import functools

import jax
import jax.numpy as jnp
from jax import lax
from jax.experimental import pallas as pl
from jax.experimental.pallas import tpu as pltpu
from jax.sharding import PartitionSpec as P

ADAPTER_SCALE = 2.0
F32 = jnp.float32
BF16 = jnp.bfloat16
LANES = 128


def swiglu_parts(gate_value, up_value):
    gate_float = gate_value.astype(F32)
    up_float = up_value.astype(F32)
    sigmoid_gate = jax.nn.sigmoid(gate_float)
    activated = gate_float * sigmoid_gate
    hidden_state = (activated * up_float).astype(BF16)
    gate_factor = up_float * sigmoid_gate * (1.0 + gate_float * (1.0 - sigmoid_gate))
    return (hidden_state, gate_factor, activated)


def whole(count):
    return [pl.BlockSpec(memory_space=pltpu.VMEM)] * count


def pack_kernel(
    cot_ref,
    routed_ref,
    routed_map_ref,
    gate_ref,
    up_ref,
    shared_map_ref,
    map_ref,
    out_ref,
    hidden_ref,
):
    n_tensor = out_ref.shape[0] // 8
    width = cot_ref.shape[1] // n_tensor
    per_expert = routed_ref.shape[2] // LANES
    experts = routed_ref.shape[0]
    inner = [
        jnp.dot(routed_map_ref[e], routed_ref[e], preferred_element_type=F32)
        for e in range(experts)
    ]
    hidden = swiglu_parts(gate_ref[...], up_ref[...])[0]
    hidden_ref[...] = hidden
    shared = lax.dot_general(
        shared_map_ref[...], hidden, (((1,), (1,)), ((), ())), preferred_element_type=F32
    )

    def chunk(t):
        if t < experts * per_expert:
            column = t % per_expert * LANES
            return inner[t // per_expert][:, column : column + LANES]
        return jnp.zeros((16, LANES), F32)

    rank = lax.dot_general(
        cot_ref[...], map_ref[...], (((1,), (1,)), ((), ())), preferred_element_type=F32
    )
    rank = jnp.concatenate([rank, jnp.zeros((8, LANES - rank.shape[1]), F32)], axis=1)
    common = [shared[0:8], shared[8:16], rank]
    common = [jnp.concatenate([x, x], axis=0).astype(BF16) for x in common]

    for pair in range(n_tensor // 2):
        rows = pl.ds(16 * pair, 16)
        both = cot_ref[:, 2 * pair * width : 2 * (pair + 1) * width].astype(F32)
        swapped = jnp.concatenate([both[:, width:], both[:, :width]], axis=1)
        out_ref[rows, 0 : 2 * width] = jnp.concatenate([both, swapped], axis=0).astype(BF16)
        first, second = chunk(2 * pair), chunk(2 * pair + 1)
        low = jnp.concatenate([first[0:8], second[0:8]], axis=0)
        high = jnp.concatenate([first[8:16], second[8:16]], axis=0)
        out_ref[rows, 2 * width : 2 * width + LANES] = low.astype(BF16)
        out_ref[rows, 2 * width + LANES : 2 * width + 2 * LANES] = high.astype(BF16)
        for n, x in enumerate(common):
            lane = 2 * width + (2 + n) * LANES
            out_ref[rows, lane : lane + LANES] = x


def dispatch_kernel(
    parity_ref,
    index_ref,
    weight_ref,
    packed_ref,
    hidden_ref,
    out_ref,
    chunk_ref,
    rank_ref,
    adapter_ref,
):
    tokens = packed_ref.shape[0]
    width = adapter_ref.shape[1] - hidden_ref.shape[1]
    top = index_ref.shape[0]
    peers = out_ref.shape[0] // 8
    own = packed_ref[:, 0:width]
    other = packed_ref[:, width : 2 * width]

    def summed(lane):
        halves = []
        for first in (lane, lane + LANES):
            partial = packed_ref[:, first : first + LANES].astype(F32)
            halves.append(jnp.sum(partial.reshape(tokens // 8, 8, LANES), axis=0))
        return jnp.concatenate(halves, axis=0).astype(BF16)

    chunk_ref[...] = summed(2 * width)
    shared_inner = summed(2 * width + 2 * LANES)
    shared_rank = packed_ref[:, 2 * width + 4 * LANES : 2 * width + 5 * LANES]
    rank_ref[...] = shared_rank
    adapter_a = lax.dot_general(
        shared_rank, hidden_ref[...], (((0,), (0,)), ((), ())), preferred_element_type=F32
    )
    adapter_ref[:, 0 : hidden_ref.shape[1]] = adapter_a[0 : adapter_ref.shape[0]]
    adapter_ref[:, hidden_ref.shape[1] :] = jnp.dot(
        shared_inner, own, preferred_element_type=F32
    )
    before = (
        lax.broadcasted_iota(jnp.int32, (tokens, tokens), 0)
        < lax.broadcasted_iota(jnp.int32, (tokens, tokens), 1)
    ).astype(BF16)
    expert = 2 * lax.broadcasted_iota(jnp.int32, (peers, tokens), 0) + parity_ref[0]
    weight = jnp.zeros((peers, tokens), F32)
    named = jnp.zeros((peers, tokens), F32)
    for k in range(top):
        match = expert == index_ref[k : k + 1, :]
        weight = jnp.where(match, weight_ref[k : k + 1, :], weight)
        named = jnp.where(match, 1.0, named)
    slot = jnp.dot(named.astype(BF16), before, preferred_element_type=F32)
    shape = (peers, 8, tokens)
    row = lax.broadcasted_iota(jnp.int32, shape, 1)
    slot = jnp.broadcast_to(slot[:, None, :], shape)
    weight = jnp.broadcast_to(weight[:, None, :], shape)

    def split(selector):
        selector = selector.reshape(peers * 8, tokens)
        high = selector.astype(BF16)
        return high, (selector - high.astype(F32)).astype(BF16)

    high, low = split(jnp.where(slot == row.astype(F32), weight, 0.0))
    left = jnp.concatenate([high, low], axis=1)
    both = packed_ref[:, 0 : 2 * width]
    right = jnp.concatenate([both, both], axis=0)
    out_ref[:, 0 : 2 * width] = jnp.dot(left, right, preferred_element_type=F32).astype(BF16)
    wanted = jnp.where(row < 4, row + 8, row + 4).astype(F32)
    tail = jnp.where(slot == wanted, weight, 0.0)
    first = split(jnp.where(row < 4, tail, 0.0))
    second = split(jnp.where(row < 4, 0.0, tail))
    left = jnp.concatenate([first[0], first[1], second[0], second[1]], axis=1)
    right = jnp.concatenate([own, own, other, other], axis=0)
    out_ref[:, 2 * width : 3 * width] = jnp.dot(left, right, preferred_element_type=F32).astype(BF16)
    rest = out_ref.shape[1] - 3 * width
    out_ref[:, 3 * width :] = jnp.zeros((peers * 8, rest), BF16)


def routed_kernel(
    hidden_local,
    parity_ref,
    arrived_ref,
    own_weight_ref,
    pair_weight_ref,
    own_map_ref,
    pair_map_ref,
    chunk_ref,
    part_ref,
    own_rows_ref,
    pair_rows_ref,
    gather_ref,
):
    slots, width = own_rows_ref.shape
    block, groups = 192, 16
    turned = (((0,), (1,)), ((), ()))

    @pl.when(pl.program_id(0) == 0)
    def _():
        i = lax.broadcasted_iota(jnp.int32, (block, 8 * groups), 0)
        j = lax.broadcasted_iota(jnp.int32, (block, 8 * groups), 1)
        group = lax.shift_right_logical(i * 5462, 16)
        slot = i - 12 * group
        head = (j == 8 * group + slot) & (slot < 8)
        for half, rows_ref in enumerate((own_rows_ref, pair_rows_ref)):
            tail = (j == 8 * group + slot - 8 + 4 * half) & (slot >= 8)
            pick = jnp.concatenate([head.astype(F32), tail.astype(F32)], axis=1).astype(BF16)
            for b in range(slots // block):
                rows = pl.ds(8 * groups * b, 8 * groups)
                source = jnp.concatenate(
                    [
                        arrived_ref[rows, half * width : (half + 1) * width],
                        arrived_ref[rows, 2 * width : 3 * width],
                    ],
                    axis=0,
                )
                rows_ref[block * b : block * (b + 1), :] = jnp.dot(
                    pick, source, preferred_element_type=F32
                ).astype(BF16)
        rank = lax.dot_general(
            own_map_ref[0], own_rows_ref[...], (((1,), (1,)), ((), ())), preferred_element_type=F32
        )
        pair_rank = lax.dot_general(
            pair_map_ref[...], pair_rows_ref[...], turned, preferred_element_type=F32
        )
        gather_ref[:, 0:slots] = (rank + pair_rank[0 : rank.shape[0]]).astype(BF16)
        gather_ref[:, slots : slots + LANES] = chunk_ref[...]

    part = lax.dot_general(
        own_weight_ref[0], own_rows_ref[...], turned, preferred_element_type=F32
    ) + lax.dot_general(
        pair_weight_ref[...], pair_rows_ref[...], turned, preferred_element_type=F32
    )
    flip = 1 - parity_ref[0]
    for b in range(part.shape[0] // hidden_local):
        start = pl.multiple_of((b ^ flip) * hidden_local, hidden_local)
        part_ref[pl.ds(start, hidden_local), :] = part[
            b * hidden_local : (b + 1) * hidden_local
        ].astype(BF16)


def shards(
    cotangent,
    routed_expert_index,
    chosen_gate_weight,
    routed_down_weight,
    routed_adapter_input_map,
    routed_adapter_output_map,
    routed_gate_saved,
    routed_up_saved,
    shared_down_weight,
    shared_adapter_input_map,
    shared_adapter_output_map,
    shared_gate_saved,
    shared_up_saved,
):
    n_tensor = lax.axis_size("tensor")
    group_count = lax.axis_size("expert") * lax.axis_size("dp")
    expert_local, expert_hidden, width = routed_down_weight.shape
    hidden_local = expert_hidden // n_tensor
    slot_count = routed_gate_saved.shape[2]
    rank_size = routed_adapter_output_map.shape[1]
    scale = ADAPTER_SCALE / group_count
    contract_trailing = (((1,), (1,)), ((), ()))
    parity = lax.bitwise_and(lax.axis_index("tensor"), 1)
    even = parity == 0
    parity_scalar = parity.reshape(1)
    swap = [(t, t ^ 1) for t in range(n_tensor)]
    same_parity = [list(range(p, n_tensor, 2)) for p in range(2)]

    def pick(array, index, size):
        return lax.dynamic_slice_in_dim(array, index * size, size, 0, allow_negative_indices=False)

    token_rows = lax.all_gather(cotangent, "tensor", axis=1, tiled=True)[0]
    tokens = token_rows.shape[0]

    routed_hidden, routed_gate_factor, routed_activated = swiglu_parts(
        routed_gate_saved, routed_up_saved
    )
    shared_local = shared_gate_saved.shape[2]
    packed, shared_hidden = pl.pallas_call(
        pack_kernel,
        out_shape=(
            jax.ShapeDtypeStruct((8 * n_tensor, 2 * width + 5 * LANES), BF16),
            jax.ShapeDtypeStruct((tokens, shared_local), BF16),
        ),
        in_specs=whole(7),
        out_specs=tuple(whole(2)),
        name="pack",
    )(
        cotangent[0],
        jnp.swapaxes(routed_hidden, 0, 1),
        jnp.swapaxes(routed_adapter_input_map, 1, 2),
        shared_gate_saved[0],
        shared_up_saved[0],
        shared_adapter_input_map.T,
        shared_adapter_output_map,
    )
    packed = lax.all_to_all(packed, "tensor", split_axis=0, concat_axis=0, tiled=True)

    block_width = -(-3 * width // LANES) * LANES
    outgoing, inner_chunk, shared_rank, adapter = pl.pallas_call(
        dispatch_kernel,
        out_shape=(
            jax.ShapeDtypeStruct((group_count * 8, block_width), BF16),
            jax.ShapeDtypeStruct((rank_size, LANES), BF16),
            jax.ShapeDtypeStruct((tokens, LANES), BF16),
            jax.ShapeDtypeStruct((rank_size, shared_local + width), F32),
        ),
        in_specs=[pl.BlockSpec(memory_space=pltpu.SMEM)] + whole(4),
        out_specs=tuple(whole(4)),
        name="dispatch",
        compiler_params=pltpu.CompilerParams(vmem_limit_bytes=32 * 1024 * 1024),
    )(parity_scalar, routed_expert_index[0].T, chosen_gate_weight[0].T, packed, shared_hidden)
    shared_rank = shared_rank[:, :rank_size]

    sent_weight = jnp.concatenate(
        [
            pick(routed_down_weight, 1 - parity, 1)[0],
            pick(routed_adapter_output_map, 1 - parity, 1)[0],
            jnp.zeros((LANES - rank_size, width), BF16),
        ],
        axis=0,
    ).T
    outgoing, sent_weight = lax.optimization_barrier((outgoing, sent_weight))
    pair_weight = lax.ppermute(sent_weight, "tensor", swap)
    arrived = lax.all_to_all(
        outgoing, ("expert", "dp"), split_axis=0, concat_axis=0, tiled=True
    )
    adapter = lax.all_gather(adapter.astype(BF16), "expert")
    adapter = jnp.sum(adapter.astype(F32), axis=0).astype(BF16)
    arrived, adapter = lax.optimization_barrier((arrived, adapter))

    steps = 4
    fan = expert_hidden // steps
    part, own_rows, pair_rows, rank_part = pl.pallas_call(
        functools.partial(routed_kernel, hidden_local),
        grid_spec=pltpu.PrefetchScalarGridSpec(
            num_scalar_prefetch=1,
            grid=(steps,),
            in_specs=[
                pl.BlockSpec((group_count * 8, block_width), lambda j, p: (0, 0)),
                pl.BlockSpec((1, width, fan), lambda j, p: (p[0], 0, j)),
                pl.BlockSpec((width, fan), lambda j, p: (0, j)),
                pl.BlockSpec((1, rank_size, width), lambda j, p: (p[0], 0, 0)),
                pl.BlockSpec((width, LANES), lambda j, p: (0, expert_hidden // LANES)),
                pl.BlockSpec((rank_size, LANES), lambda j, p: (0, 0)),
            ],
            out_specs=(
                pl.BlockSpec((fan, slot_count), lambda j, p: (j, 0)),
                pl.BlockSpec((slot_count, width), lambda j, p: (0, 0)),
                pl.BlockSpec((slot_count, width), lambda j, p: (0, 0)),
                pl.BlockSpec((rank_size, slot_count + LANES), lambda j, p: (0, 0)),
            ),
        ),
        out_shape=(
            pltpu.HBM((expert_hidden, slot_count), BF16),
            pltpu.HBM((slot_count, width), BF16),
            pltpu.HBM((slot_count, width), BF16),
            jax.ShapeDtypeStruct((rank_size, slot_count + LANES), BF16),
        ),
        name="routed",
        compiler_params=pltpu.CompilerParams(vmem_limit_bytes=48 * 1024 * 1024),
    )(
        parity_scalar,
        arrived,
        jnp.swapaxes(routed_down_weight, 1, 2),
        pair_weight,
        routed_adapter_output_map,
        pair_weight,
        inner_chunk,
    )
    part, rank_part, token_rows, adapter = lax.optimization_barrier(
        (part, rank_part, token_rows, adapter)
    )
    reduced = lax.psum_scatter(
        part, "tensor", scatter_dimension=0, axis_index_groups=same_parity, tiled=True
    )
    taken = lax.ppermute(reduced[:hidden_local], "tensor", swap)
    kept = reduced[hidden_local:]
    hidden_gradient = jnp.stack(
        [jnp.where(even, kept, taken), jnp.where(even, taken, kept)], axis=1
    )

    gathered = lax.all_gather(rank_part, "tensor", axis=0, tiled=True).reshape(
        n_tensor, rank_size, -1
    )
    adapter = scale * jnp.sum(lax.all_gather(adapter, "dp").astype(F32), axis=0)
    grad_a_shared = adapter[:, :shared_local].T
    grad_b_shared = adapter[:, shared_local:]
    routed_rank = jnp.sum(
        gathered[:, :, :slot_count]
        .reshape(n_tensor // 2, expert_local, rank_size, slot_count)
        .astype(F32),
        axis=0,
    ).astype(BF16)
    chunks = slot_count // LANES
    inner_chunks = gathered[:, :, slot_count:]
    own_inner = pick(inner_chunks, parity, chunks)
    own_inner = jnp.swapaxes(own_inner, 0, 1).reshape(rank_size, slot_count)
    _, shared_gate_factor, shared_activated = swiglu_parts(
        shared_gate_saved[0], shared_up_saved[0]
    )
    shared_gradient = lax.dot_general(
        token_rows, shared_down_weight, contract_trailing, preferred_element_type=F32
    )
    shared_gradient = shared_gradient + ADAPTER_SCALE * lax.dot_general(
        shared_rank, shared_adapter_input_map, contract_trailing, preferred_element_type=F32
    )
    grad_gate_shared = (shared_gradient * shared_gate_factor).astype(BF16)[None]
    grad_up_shared = (shared_gradient * shared_activated).astype(BF16)[None]

    grad_a_routed = scale * jnp.einsum(
        "fes,ers->efr", routed_hidden, routed_rank, preferred_element_type=F32
    )
    own_b = scale * jnp.dot(own_inner, own_rows, preferred_element_type=F32)
    pair_b = scale * jnp.dot(own_inner, pair_rows, preferred_element_type=F32)
    pair_b = lax.ppermute(pair_b, "tensor", swap)
    grad_b_routed = jnp.stack([jnp.where(even, own_b, pair_b), jnp.where(even, pair_b, own_b)])
    low_rank = ADAPTER_SCALE * jnp.einsum(
        "ers,efr->fes", routed_rank, routed_adapter_input_map, preferred_element_type=F32
    )
    hidden_gradient = hidden_gradient.astype(F32) + low_rank
    grad_gate_routed = (hidden_gradient * routed_gate_factor).astype(BF16)
    grad_up_routed = (hidden_gradient * routed_activated).astype(BF16)
    return (
        grad_gate_routed,
        grad_up_routed,
        grad_gate_shared,
        grad_up_shared,
        grad_a_routed,
        grad_b_routed,
        grad_a_shared,
        grad_b_shared,
    )


def solution(mesh):
    placed = (
        P(("expert", "dp"), "tensor", None),
        P(("expert", "dp"), None, None),
        P(("expert", "dp"), None, None),
        P(("expert", "dp"), None, "tensor"),
        P(("expert", "dp"), "tensor", None),
        P(("expert", "dp"), None, "tensor"),
        P("tensor", ("expert", "dp"), None),
        P("tensor", ("expert", "dp"), None),
        P("tensor", None),
        P("tensor", None),
        P(),
        P(("expert", "dp"), None, "tensor"),
        P(("expert", "dp"), None, "tensor"),
    )
    return jax.shard_map(
        shards,
        mesh=mesh,
        in_specs=placed,
        out_specs=(
            P("tensor", ("expert", "dp"), None),
            P("tensor", ("expert", "dp"), None),
            P(("expert", "dp"), None, "tensor"),
            P(("expert", "dp"), None, "tensor"),
            P(("expert", "dp"), "tensor", None),
            P(("expert", "dp"), None, "tensor"),
            P("tensor", None),
            P(None, "tensor"),
        ),
        check_vma=False,
    )
```

profile of v0, /device:TPU:16, one launch (start us, length us, event | category | flops | bytes accessed | tf_op | source)
XLA Modules:
  0.0 198.5 jit_solution(15102032151163335158)
XLA Ops:
  7.2 0.0 copy-start
  7.2 2.0 fusion.2
  9.2 2.2 %pack.1 = (bf16[128,1536]{1,0:T(8,128)(2,1)}, bf16[128,128]{1,0:T(8,128)(2,1)}) custom-call(bf16[8,7168]{1,0:T(8,128)(2,1)} %bitcast.78, bf16[2,64,768]{2,1,0:T(8,128)(2,1)} %bitcast.74, bf16[2,16,64]{2,1,0:T(8,128)(2,1)} %bitcast.86, bf16[128,128]{1,0:T(8,128)(2,1)} %bitcast.84, bf16[128,128]{1,0:T(8,128)(2,1)} %bitcast.85, bf16[16,128]{1,0:T(8,128)(2,1)} %bitcast.87, ...), custom_call_target="tpu_custom_call" | custom-call | tf_op jit(solution)/shard_map/pack/pallas_call | solution.py:258
  11.4 18.9 %all-to-all-start = ((bf16[16,8,1536]{2,1,0:T(8,128)(2,1)}), bf16[16,8,1536]{2,1,0:T(8,128)(2,1)S(1)}, u32[]{:S(2)}, u32[]{:S(2)}) async-start(bf16[16,8,1536]{2,1,0:T(8,128)(2,1)} %bitcast.80), calls=%async_computation | async-start | bytes 786432 | tf_op jit(solution)/shard_map/all_to_all | solution.py:276
  30.2 0.0 all-gather.4.cloned.1.call-start
  30.3 0.7 all-gather.4.cloned.1.call-update
  31.0 0.1 copy.34
  31.1 0.0 copy-start.4
  31.1 0.0 copy-start.5
  31.2 0.0 copy-start.6
  31.2 1.3 dynamic-slice_bitcast_fusion
  32.5 1.9 concatenate.3
  34.4 19.6 %all-to-all-done = bf16[16,8,1536]{2,1,0:T(8,128)(2,1)S(1)} async-done(((bf16[16,8,1536]{2,1,0:T(8,128)(2,1)}), bf16[16,8,1536]{2,1,0:T(8,128)(2,1)S(1)}, u32[]{:S(2)}, u32[]{:S(2)}) %all-to-all-start) | async-done | bytes 393248 | tf_op jit(solution)/shard_map/all_to_all | solution.py:276
  54.0 0.9 dispatch.1
  54.9 1.1 copy-done.2
  56.0 10.5 %all-to-all-start.1 = ((bf16[64,8,1408]{2,1,0:T(8,128)(2,1)}), bf16[64,8,1408]{2,1,0:T(8,128)(2,1)S(1)}, u32[]{:S(2)}, u32[]{:S(2)}) async-start(bf16[64,8,1408]{2,1,0:T(8,128)(2,1)} %bitcast.68), calls=%async_computation.1 | async-start | bytes 2883584 | tf_op jit(solution)/shard_map/all_to_all | solution.py:304
  66.5 0.0 reduce-scatter.2.cloned.1.call-start
  66.5 1.9 collective-permute-start
  68.5 43.9 %all-gather = bf16[256,576]{1,0:T(8,128)(2,1)} all-gather(bf16[16,576]{1,0:T(8,128)(2,1)S(1)} %convert_element_type.43), channel_id=2, replica_groups=mesh['expert'=16,'tensor'=16,'dp'=4] {'expert'}, dimensions={0}, use_global_device_ids=true | all-gather | bytes 313344 | tf_op jit(solution)/shard_map/all_gather | solution.py:307
  112.4 1.0 reduce_sum.33
  113.4 0.0 all-to-all-done.1
  113.5 0.0 copy-start.1
  113.5 1.5 copy-done.1
  115.0 6.1 %routed.1 = (bf16[1024,768]{1,0:T(8,128)(2,1)}, bf16[768,448]{1,0:T(8,128)(2,1)}, bf16[768,448]{1,0:T(8,128)(2,1)}, bf16[16,896]{1,0:T(8,128)(2,1)S(1)}) custom-call(s32[1]{0:T(128)} %bitcast.parity_ref, bf16[512,1408]{1,0:T(8,128)(2,1)S(1)} %bitcast.65, bf16[2,448,1024]{2,1,0:T(8,128)(2,1)S(1)} %bitcast.66, ...), custom_call_target="tpu_custom_call" | custom-call | tf_op jit(solution)/shard_map/routed/pallas_call | solution.py:313
  121.0 0.0 reduce-scatter.2.cloned.1.call-update
  121.1 0.0 copy-start.7
  121.1 37.4 %all_gather.21 = bf16[256,896]{1,0:T(8,128)(2,1)S(1)} all-gather(bf16[16,896]{1,0:T(8,128)(2,1)S(1)} %get-tuple-element.38), channel_id=1, replica_groups=mesh['expert'=16,'tensor'=16,'dp'=4] {'tensor'}, dimensions={0}, use_global_device_ids=true | all-gather | bytes 487424 | tf_op jit(solution)/shard_map/all_gather | solution.py:362
  158.6 0.2 convolution_multiply_fusion.2
  158.8 5.0 %collective-permute-start.2 = (f32[16,448]{1,0:T(8,128)S(1)}, f32[16,448]{1,0:T(8,128)S(1)}, u32[]{:S(2)}, u32[]{:S(2)}) collective-permute-start(f32[16,448]{1,0:T(8,128)S(1)} %convolution_multiply_fusion.2), channel_id=1, source_target_pairs={{0,4},{4,0},{8,12},{12,8},{16,20},{20,16},{24,28},{28,24},{32,36},... | collective-permute-start | bytes 86024 | tf_op jit(solution)/shard_map/ppermute | solution.py:395
  163.8 0.1 reduce_sum.34
  163.9 12.0 %all-gather.1 = bf16[64,576]{1,0:T(8,128)(2,1)S(1)} all-gather(bf16[16,576]{1,0:T(8,128)(2,1)S(1)} %reduce_sum.33), channel_id=3, replica_groups=mesh['expert'=16,'tensor'=16,'dp'=4] {'dp'}, dimensions={0}, use_global_device_ids=true | all-gather | bytes 92160 | tf_op jit(solution)/shard_map/all_gather | solution.py:365
  175.9 0.6 slice_bitcast_fusion
  176.5 0.8 convolution_multiply_fusion.4
  177.3 2.2 %fusion.30 = f32[128,128]{1,0:T(8,128)S(1)} fusion(bf16[128,7168]{1,0:T(8,128)(2,1)} %bitcast.71, bf16[128,7168]{1,0:T(8,128)(2,1)S(1)} %copy-done), kind=kOutput, calls=%fused_computation.53 | convolution fusion | flops 234881024 | bytes 3735552 | tf_op jit(solution)/shard_map/dot_general | solution.py:381
  179.6 0.0 copy-start.10
  179.6 0.0 copy-start.11
  179.6 0.0 copy-start.14
  179.6 0.8 fusion.20
  180.4 0.6 slice.33
  181.0 0.2 select_bitcast_fusion.3
  181.2 0.9 slice.29
  182.1 1.9 collective-permute-start.1
  184.1 0.6 pad_maximum_fusion.1
  184.7 3.9 %collective-permute-done.1 = bf16[64,768]{1,0:T(8,128)(2,1)S(1)} collective-permute-done((bf16[64,768]{1,0:T(8,128)(2,1)S(1)}, bf16[64,768]{1,0:T(8,128)(2,1)S(1)}, u32[]{:S(2)}, u32[]{:S(2)}) %collective-permute-start.1) | collective-permute-done | bytes 98336 | tf_op jit(solution)/shard_map/ppermute | solution.py:356
  188.6 0.9 select_bitcast_fusion.1
  189.6 0.4 multiply_convert_fusion
  189.9 0.9 copy.36
  190.8 0.9 copy.37
  (34 shorter events, 0.2 us)
Async XLA Ops:
  7.2 170.1 %copy-start = (bf16[128,7168]{1,0:T(8,128)(2,1)S(1)}, bf16[128,7168]{1,0:T(8,128)(2,1)}, u32[]{:S(2)}) copy-start(bf16[128,7168]{1,0:T(8,128)(2,1)} %param.21) | copy-start | bytes 5505028
  7.2 23.8 %copy-start.3 = (bf16[2,16,448]{2,1,0:T(8,128)(2,1)S(1)}, bf16[2,16,448]{2,1,0:T(8,128)(2,1)}, u32[]{:S(2)}) copy-start(bf16[2,16,448]{2,1,0:T(8,128)(2,1)} %own_map_ref.1) | copy-start | bytes 86020
  11.4 42.6 %all-to-all-start = ((bf16[16,8,1536]{2,1,0:T(8,128)(2,1)}), bf16[16,8,1536]{2,1,0:T(8,128)(2,1)S(1)}, u32[]{:S(2)}, u32[]{:S(2)}) async-start(bf16[16,8,1536]{2,1,0:T(8,128)(2,1)} %bitcast.80), calls=%async_computation | async-start | bytes 786432 | tf_op jit(solution)/shard_map/all_to_all | solution.py:276
  30.2 90.8 %all-gather.4.cloned.1.call-start = ((), (), s32[]{:S(2)}) async-start(), calls=%async_computation.3 | async-start | bytes 1949696 | tf_op jit(solution)/shard_map/all_gather | solution.py:251
  31.1 22.9 %copy-start.4 = (bf16[128,128]{1,0:T(8,128)(2,1)S(1)}, bf16[128,128]{1,0:T(8,128)(2,1)}, u32[]{:S(2)}) copy-start(bf16[128,128]{1,0:T(8,128)(2,1)} %get-tuple-element.27.hidden_ref) | copy-start | bytes 98308
  31.1 22.9 %copy-start.5 = (s32[1,128,8]{1,2,0:T(8,128)S(1)}, s32[1,128,8]{1,2,0:T(8,128)}, u32[]{:S(2)}) copy-start(s32[1,128,8]{1,2,0:T(8,128)} %param.14) | copy-start | bytes 12292
  31.2 22.8 %copy-start.6 = (f32[1,128,8]{1,2,0:T(8,128)S(1)}, f32[1,128,8]{1,2,0:T(8,128)}, u32[]{:S(2)}) copy-start(f32[1,128,8]{1,2,0:T(8,128)} %param.15) | copy-start | bytes 12292
  54.9 1.1 copy-start.2
  56.0 57.5 %all-to-all-start.1 = ((bf16[64,8,1408]{2,1,0:T(8,128)(2,1)}), bf16[64,8,1408]{2,1,0:T(8,128)(2,1)S(1)}, u32[]{:S(2)}, u32[]{:S(2)}) async-start(bf16[64,8,1408]{2,1,0:T(8,128)(2,1)} %bitcast.68), calls=%async_computation.1 | async-start | bytes 2883584 | tf_op jit(solution)/shard_map/all_to_all | solution.py:304
  66.5 114.8 %reduce-scatter.2.cloned.1.call-start = ((), (), s32[]{:S(2)}) async-start(), calls=%async_computation.4 | async-start | bytes 1769472 | tf_op jit(solution)/shard_map/reduce_scatter | solution.py:353
  66.5 47.0 %collective-permute-start = (bf16[448,1152]{1,0:T(8,128)(2,1)}, bf16[448,1152]{1,0:T(8,128)(2,1)}, u32[]{:S(2)}, u32[]{:S(2)}) collective-permute-start(bf16[448,1152]{1,0:T(8,128)(2,1)} %bitcast.77), channel_id=1, source_target_pairs={{0,4},{4,0},{8,12},{12,8},{16,20},{20,16},{24,28},{28,24},{32,36},... | collective-permute-start | bytes 3096584 | tf_op jit(solution)/shard_map/ppermute | solution.py:303
  113.5 1.5 copy-start.1
  121.0 37.5 %copy-start.9 = (bf16[768,448]{1,0:T(8,128)(2,1)S(1)}, bf16[768,448]{1,0:T(8,128)(2,1)}, u32[]{:S(2)}) copy-start(bf16[768,448]{1,0:T(8,128)(2,1)} %get-tuple-element.42) | copy-start | bytes 2064388
  121.1 55.5 %copy-start.7 = (bf16[64,2,768]{2,0,1:T(8,128)(2,1)S(1)}, bf16[64,2,768]{2,0,1:T(8,128)(2,1)}, u32[]{:S(2)}) copy-start(bf16[64,2,768]{2,0,1:T(8,128)(2,1)} %fusion.2) | copy-start | bytes 589828
  158.8 22.2 %collective-permute-start.2 = (f32[16,448]{1,0:T(8,128)S(1)}, f32[16,448]{1,0:T(8,128)S(1)}, u32[]{:S(2)}, u32[]{:S(2)}) collective-permute-start(f32[16,448]{1,0:T(8,128)S(1)} %convolution_multiply_fusion.2), channel_id=1, source_target_pairs={{0,4},{4,0},{8,12},{12,8},{16,20},{20,16},{24,28},{28,24},{32,36},... | collective-permute-start | bytes 86024 | tf_op jit(solution)/shard_map/ppermute | solution.py:395
  177.3 2.3 %copy-start.12 = (bf16[1,128,128]{2,1,0:T(8,128)(2,1)S(1)}, bf16[1,128,128]{2,1,0:T(8,128)(2,1)}, u32[]{:S(2)}) copy-start(bf16[1,128,128]{2,1,0:T(8,128)(2,1)} %param.24) | copy-start | bytes 98308
  177.3 2.3 %copy-start.13 = (bf16[1,128,128]{2,1,0:T(8,128)(2,1)S(1)}, bf16[1,128,128]{2,1,0:T(8,128)(2,1)}, u32[]{:S(2)}) copy-start(bf16[1,128,128]{2,1,0:T(8,128)(2,1)} %param.25) | copy-start | bytes 98308
  177.3 2.3 %copy-start.15 = (bf16[128,16]{0,1:T(8,128)(2,1)S(1)}, bf16[128,16]{0,1:T(8,128)(2,1)}, u32[]{:S(2)}) copy-start(bf16[128,16]{0,1:T(8,128)(2,1)} %param.22) | copy-start | bytes 12292
  177.3 3.7 %copy-start.8 = (bf16[768,448]{1,0:T(8,128)(2,1)S(1)}, bf16[768,448]{1,0:T(8,128)(2,1)}, u32[]{:S(2)}) copy-start(bf16[768,448]{1,0:T(8,128)(2,1)} %get-tuple-element.41) | copy-start | bytes 2064388
  179.6 10.0 %copy-start.10 = (bf16[64,2,768]{2,1,0:T(2,128)(2,1)S(1)}, bf16[64,2,768]{2,1,0:T(2,128)(2,1)}, u32[]{:S(2)}) copy-start(bf16[64,2,768]{2,1,0:T(2,128)(2,1)} %param.19) | copy-start | bytes 589828
  179.6 10.0 %copy-start.11 = (bf16[64,2,768]{2,1,0:T(2,128)(2,1)S(1)}, bf16[64,2,768]{2,1,0:T(2,128)(2,1)}, u32[]{:S(2)}) copy-start(bf16[64,2,768]{2,1,0:T(2,128)(2,1)} %param.20) | copy-start | bytes 589828
  179.6 10.0 %copy-start.14 = (bf16[2,64,16]{1,2,0:T(8,128)(2,1)S(1)}, bf16[2,64,16]{1,2,0:T(8,128)(2,1)}, u32[]{:S(2)}) copy-start(bf16[2,64,16]{1,2,0:T(8,128)(2,1)} %param.17) | copy-start | bytes 12292
  182.1 6.5 %collective-permute-start.1 = (bf16[64,768]{1,0:T(8,128)(2,1)S(1)}, bf16[64,768]{1,0:T(8,128)(2,1)S(1)}, u32[]{:S(2)}, u32[]{:S(2)}) collective-permute-start(bf16[64,768]{1,0:T(8,128)(2,1)S(1)} %slice.29), channel_id=1, source_target_pairs={{0,4},{4,0},{8,12},{12,8},{16,20},{20,16},{24,28},{28,24},{32,36},... | collective-permute-start | bytes 294920 | tf_op jit(solution)/shard_map/ppermute | solution.py:356
Sparse Core Ops, SparseCore 0:
  33.7 78.8 all-gather.3
  121.2 56.8 reduce-scatter.1
where the time goes:
time: 199 us
  blocking collectives  93.4 us (47%)
  starting transfers between devices  38.3 us (19%)
  waiting for transfers between devices  24.3 us (12%)
  between operations  14.4 us (7%)
  local copies, waits for them, and re-layouts  9.97 us (5%)
  Pallas kernels  9.13 us (5%)
  other arithmetic  4.62 us (2%)
  matrix products  4.54 us (2%)
    all_gather x1, blocking collectives, shards(): adapter = lax.all_gather(adapter.astype(BF16), 'expert')  43.9 us
    all_gather x1, blocking collectives, shards(): lax.all_gather(rank_part, 'tensor', axis=0, tiled=True)  37.4 us
    all_to_all x1, waiting for transfers between devices, shards(): lax.all_to_all(packed, 'tensor', split_axis=0, concat_axis=0, tiled=True)  19.6 us
    all_to_all x1, starting transfers between devices, shards(): lax.all_to_all(packed, 'tensor', split_axis=0, concat_axis=0, tiled=True)  18.9 us
    all_gather x1, blocking collectives, shards(): adapter = scale * jnp.sum(lax.all_gather(adapter, 'dp').astype(F32), axis=0)  12 us
    all_to_all x1, starting transfers between devices, shards(): lax.all_to_all(outgoing, ('expert', 'dp'), split_axis=0, concat_axis=0, t...  10.5 us
    pallas_call x1, Pallas kernels, shards(): pl.pallas_call(functools.partial(routed_kernel, hidden_local), grid_spec=...  6.07 us
    ppermute x1, starting transfers between devices, shards(): pair_b = lax.ppermute(pair_b, 'tensor', swap)  5.02 us
  transfers between devices with their start and end apart: 7, of which 2 were waited for; matrix products, arithmetic and copies ran while one was open for 5% of the time, Pallas kernels for 3%

commit v1 on v0

--- a/solution.py
+++ b/solution.py
@@ -53,9 +53,9 @@
     )
 
     def chunk(t):
-        if t < experts * per_expert:
-            column = t % per_expert * LANES
-            return inner[t // per_expert][:, column : column + LANES]
+        if t // experts < per_expert:
+            column = t // experts * LANES
+            return inner[t % experts][:, column : column + LANES]
         return jnp.zeros((16, LANES), F32)
 
     rank = lax.dot_general(
@@ -304,7 +304,7 @@
     arrived = lax.all_to_all(
         outgoing, ("expert", "dp"), split_axis=0, concat_axis=0, tiled=True
     )
-    adapter = lax.all_gather(adapter.astype(BF16), "expert")
+    adapter = lax.all_gather(adapter.astype(BF16), "dp")
     adapter = jnp.sum(adapter.astype(F32), axis=0).astype(BF16)
     arrived, adapter = lax.optimization_barrier((arrived, adapter))
 
@@ -359,22 +359,26 @@
         [jnp.where(even, kept, taken), jnp.where(even, taken, kept)], axis=1
     )
 
-    gathered = lax.all_gather(rank_part, "tensor", axis=0, tiled=True).reshape(
-        n_tensor, rank_size, -1
-    )
-    adapter = scale * jnp.sum(lax.all_gather(adapter, "dp").astype(F32), axis=0)
+    gathered = lax.all_gather(
+        rank_part, "tensor", axis=0, axis_index_groups=same_parity, tiled=True
+    ).reshape(n_tensor // 2, rank_size, -1)
+    own_rank = jnp.sum(gathered[:, :, :slot_count].astype(F32), axis=0).astype(BF16)
+    own_inner = jnp.swapaxes(gathered[: slot_count // LANES, :, slot_count:], 0, 1)
+    own_inner = own_inner.reshape(rank_size, slot_count)
+    own_b = scale * jnp.dot(own_inner, own_rows, preferred_element_type=F32)
+    pair_b = scale * jnp.dot(own_inner, pair_rows, preferred_element_type=F32)
+    swapped = jnp.concatenate([own_rank, pair_b.astype(BF16)], axis=1)
+    swapped = lax.ppermute(swapped, "tensor", swap)
+    pair_rank, pair_b = swapped[:, :slot_count], swapped[:, slot_count:].astype(F32)
+    routed_rank = jnp.stack(
+        [jnp.where(even, own_rank, pair_rank), jnp.where(even, pair_rank, own_rank)]
+    )
+    grad_b_routed = jnp.stack([jnp.where(even, own_b, pair_b), jnp.where(even, pair_b, own_b)])
+
+    adapter = scale * jnp.sum(lax.all_gather(adapter, "expert").astype(F32), axis=0)
     grad_a_shared = adapter[:, :shared_local].T
     grad_b_shared = adapter[:, shared_local:]
-    routed_rank = jnp.sum(
-        gathered[:, :, :slot_count]
-        .reshape(n_tensor // 2, expert_local, rank_size, slot_count)
-        .astype(F32),
-        axis=0,
-    ).astype(BF16)
-    chunks = slot_count // LANES
-    inner_chunks = gathered[:, :, slot_count:]
-    own_inner = pick(inner_chunks, parity, chunks)
-    own_inner = jnp.swapaxes(own_inner, 0, 1).reshape(rank_size, slot_count)
+
     _, shared_gate_factor, shared_activated = swiglu_parts(
         shared_gate_saved[0], shared_up_saved[0]
     )
@@ -390,10 +394,6 @@
     grad_a_routed = scale * jnp.einsum(
         "fes,ers->efr", routed_hidden, routed_rank, preferred_element_type=F32
     )
-    own_b = scale * jnp.dot(own_inner, own_rows, preferred_element_type=F32)
-    pair_b = scale * jnp.dot(own_inner, pair_rows, preferred_element_type=F32)
-    pair_b = lax.ppermute(pair_b, "tensor", swap)
-    grad_b_routed = jnp.stack([jnp.where(even, own_b, pair_b), jnp.where(even, pair_b, own_b)])
     low_rank = ADAPTER_SCALE * jnp.einsum(
         "ers,efr->fes", routed_rank, routed_adapter_input_map, preferred_element_type=F32
     )

time: 199 us -> 193 us (0.970)
  the two profiles are of different devices: /device:TPU:16 before, /device:TPU:1 now
where the time goes in v1:
time: 193 us; the launch traced here: 190 us
  blocking collectives  61.9 us (32%)
  waiting for transfers between devices  44.9 us (23%)
  starting transfers between devices  43.5 us (23%)
  between operations  14.4 us (7%)
  local copies, waits for them, and re-layouts  9.95 us (5%)
  Pallas kernels  9.13 us (5%)
  other arithmetic  3.66 us (2%)
  matrix products  2.97 us (2%)
    all_gather x1, blocking collectives, shards(): lax.all_gather(rank_part, 'tensor', axis=0, axis_index_groups=same_parity...  25.9 us
    all_gather x1, blocking collectives, shards(): lax.all_gather(adapter, 'expert').astype(F32)  24.9 us
    all_to_all x1, waiting for transfers between devices, shards(): lax.all_to_all(outgoing, ('expert', 'dp'), split_axis=0, concat_axis=0, t...  23 us
    all_to_all x1, starting transfers between devices, shards(): lax.all_to_all(packed, 'tensor', split_axis=0, concat_axis=0, tiled=True)  19.4 us
    all_to_all x1, starting transfers between devices, shards(): lax.all_to_all(outgoing, ('expert', 'dp'), split_axis=0, concat_axis=0, t...  16.8 us
    all_to_all x1, waiting for transfers between devices, shards(): lax.all_to_all(packed, 'tensor', split_axis=0, concat_axis=0, tiled=True)  13.9 us
    all_gather x1, blocking collectives, shards(): adapter = lax.all_gather(adapter.astype(BF16), 'dp')  11.1 us
    pallas_call x1, Pallas kernels, shards(): pl.pallas_call(functools.partial(routed_kernel, hidden_local), grid_spec=...  6.08 us
  transfers between devices with their start and end apart: 7, of which 5 were waited for; matrix products, arithmetic and copies ran while one was open for 4% of the time, Pallas kernels for 4%

profile of v1, /device:TPU:1, one launch (start us, length us, event | category | flops | bytes accessed | tf_op | source)
XLA Modules:
  0.0 190.4 jit_solution(16161483620391370785)
XLA Ops:
  7.2 0.0 copy-start
  7.2 2.0 %fusion.3 = bf16[64,2,768]{2,0,1:T(8,128)(2,1)} fusion(bf16[64,2,768]{2,1,0:T(2,128)(2,1)} %param.20, bf16[64,2,768]{2,1,0:T(2,128)(2,1)} %param.19), kind=kLoop, calls=%fused_computation.15 | loop fusion | flops 786432 | bytes 589824 | tf_op jit(solution)/shard_map/convert_element_type | solution.py:21
  9.2 2.2 %pack.1 = (bf16[128,1536]{1,0:T(8,128)(2,1)}, bf16[128,128]{1,0:T(8,128)(2,1)}) custom-call(bf16[8,7168]{1,0:T(8,128)(2,1)} %bitcast.78, bf16[2,64,768]{2,1,0:T(8,128)(2,1)} %bitcast.73, bf16[2,16,64]{2,1,0:T(8,128)(2,1)} %bitcast.86, bf16[128,128]{1,0:T(8,128)(2,1)} %bitcast.84, bf16[128,128]{1,0:T(8,128)(2,1)} %bitcast.85, bf16[16,128]{1,0:T(8,128)(2,1)} %bitcast.87, ...), custom_call_target="tpu_custom_call" | custom-call | tf_op jit(solution)/shard_map/pack/pallas_call | solution.py:258
  11.3 19.4 %all-to-all-start = ((bf16[16,8,1536]{2,1,0:T(8,128)(2,1)}), bf16[16,8,1536]{2,1,0:T(8,128)(2,1)S(1)}, u32[]{:S(2)}, u32[]{:S(2)}) async-start(bf16[16,8,1536]{2,1,0:T(8,128)(2,1)} %bitcast.80), calls=%async_computation | async-start | bytes 786432 | tf_op jit(solution)/shard_map/all_to_all | solution.py:276
  30.8 0.0 all-gather.4.cloned.1.call-start
  30.8 0.7 all-gather.4.cloned.1.call-update
  31.5 0.1 copy.34
  31.7 0.0 copy-start.5
  31.7 0.0 copy-start.6
  31.7 1.3 dynamic-slice_bitcast_fusion
  33.0 1.9 %concatenate.6 = bf16[1152,448]{0,1:T(8,128)(2,1)} concatenate(bf16[1024,448]{0,1:T(8,128)(2,1)S(1)} %dynamic-slice_bitcast_fusion, bf16[16,448]{0,1:T(8,128)(2,1)S(1)} %bitcast.79, bf16[112,448]{0,1:T(8,128)(2,1)S(1)} %broadcast_in_dim.9), dimensions={0} | concatenate | bytes 2064384 | tf_op jit(solution)/shard_map/concatenate | solution.py:294
  34.9 13.9 %all-to-all-done = bf16[16,8,1536]{2,1,0:T(8,128)(2,1)S(1)} async-done(((bf16[16,8,1536]{2,1,0:T(8,128)(2,1)}), bf16[16,8,1536]{2,1,0:T(8,128)(2,1)S(1)}, u32[]{:S(2)}, u32[]{:S(2)}) %all-to-all-start) | async-done | bytes 393248 | tf_op jit(solution)/shard_map/all_to_all | solution.py:276
  48.8 0.9 dispatch.1
  49.7 1.1 copy-done.2
  50.8 16.8 %all-to-all-start.1 = ((bf16[64,8,1408]{2,1,0:T(8,128)(2,1)}), bf16[64,8,1408]{2,1,0:T(8,128)(2,1)S(1)}, u32[]{:S(2)}, u32[]{:S(2)}) async-start(bf16[64,8,1408]{2,1,0:T(8,128)(2,1)} %bitcast.69), calls=%async_computation.1 | async-start | bytes 2883584 | tf_op jit(solution)/shard_map/all_to_all | solution.py:304
  67.6 0.0 reduce-scatter.2.cloned.1.call-start
  67.7 1.9 %collective-permute-start = (bf16[448,1152]{1,0:T(8,128)(2,1)}, bf16[448,1152]{1,0:T(8,128)(2,1)}, u32[]{:S(2)}, u32[]{:S(2)}) collective-permute-start(bf16[448,1152]{1,0:T(8,128)(2,1)} %bitcast.75), channel_id=1, source_target_pairs={{0,4},{4,0},{8,12},{12,8},{16,20},{20,16},{24,28},{28,24},{32,36},... | collective-permute-start | bytes 3096584 | tf_op jit(solution)/shard_map/ppermute | solution.py:303
  69.6 11.1 %all-gather = bf16[64,576]{1,0:T(8,128)(2,1)S(1)} all-gather(bf16[16,576]{1,0:T(8,128)(2,1)S(1)} %convert_element_type.49), channel_id=2, replica_groups=mesh['expert'=16,'tensor'=16,'dp'=4] {'dp'}, dimensions={0}, use_global_device_ids=true | all-gather | bytes 92160 | tf_op jit(solution)/shard_map/all_gather | solution.py:307
  80.7 23.0 %all-to-all-done.1 = bf16[64,8,1408]{2,1,0:T(8,128)(2,1)S(1)} async-done(((bf16[64,8,1408]{2,1,0:T(8,128)(2,1)}), bf16[64,8,1408]{2,1,0:T(8,128)(2,1)S(1)}, u32[]{:S(2)}, u32[]{:S(2)}) %all-to-all-start.1) | async-done | bytes 1441824 | tf_op jit(solution)/shard_map/all_to_all | solution.py:304
  103.8 1.4 collective-permute-done.pair_weight_ref.pair_map_ref
  105.2 1.5 copy-done.1
  106.7 6.1 %routed.1 = (bf16[1024,768]{1,0:T(8,128)(2,1)}, bf16[768,448]{1,0:T(8,128)(2,1)}, bf16[768,448]{1,0:T(8,128)(2,1)}, bf16[16,896]{1,0:T(8,128)(2,1)S(1)}) custom-call(s32[1]{0:T(128)} %bitcast.parity_ref, bf16[512,1408]{1,0:T(8,128)(2,1)S(1)} %bitcast.66, bf16[2,448,1024]{2,1,0:T(8,128)(2,1)S(1)} %bitcast.67, ...), custom_call_target="tpu_custom_call" | custom-call | tf_op jit(solution)/shard_map/routed/pallas_call | solution.py:313
  112.8 0.0 reduce-scatter.2.cloned.1.call-update
  112.8 25.9 %all_gather.21 = bf16[128,896]{1,0:T(8,128)(2,1)S(1)} all-gather(bf16[16,896]{1,0:T(8,128)(2,1)S(1)} %get-tuple-element.38), channel_id=1, replica_groups={{0,8,16,24,32,40,48,56},{4,12,20,28,36,44,52,60},{1,9,17,25,33,41,49,57..., dimensions={0}, use_global_device_ids=true | all-gather | bytes 258048 | tf_op jit(solution)/shard_map/all_gather | solution.py:362
  138.7 0.2 fusion.2
  139.0 3.4 %collective-permute-start.2 = (bf16[16,1216]{1,0:T(8,128)(2,1)S(1)}, bf16[16,1216]{1,0:T(8,128)(2,1)S(1)}, u32[]{:S(2)}, u32[]{:S(2)}) collective-permute-start(bf16[16,1216]{1,0:T(8,128)(2,1)S(1)} %pad_maximum_fusion.3), channel_id=1, source_target_pairs={{0,4},{4,0},{8,12},{12,8},{16,20},{20,16},{24,28},{28,24},{32,36},... | collective-permute-start | bytes 116744 | tf_op jit(solution)/shard_map/ppermute | solution.py:371
  142.3 24.9 %all-gather.1 = bf16[256,576]{1,0:T(8,128)(2,1)S(1)} all-gather(bf16[16,576]{1,0:T(8,128)(2,1)S(1)} %reduce_sum.33), channel_id=3, replica_groups=mesh['expert'=16,'tensor'=16,'dp'=4] {'expert'}, dimensions={0}, use_global_device_ids=true | all-gather | bytes 313344 | tf_op jit(solution)/shard_map/all_gather | solution.py:378
  167.2 0.1 convert_reduce_fusion
  167.3 0.6 slice_bitcast_fusion
  167.9 0.0 copy-start.16
  168.0 0.7 fusion.35
  168.6 0.0 copy-start.12
  168.7 0.0 copy-start.15
  168.7 0.0 copy-done.13
  168.7 0.0 copy-done.14
  168.7 0.8 fusion.23
  169.5 0.6 slice.43
  170.1 0.2 fusion.20
  170.3 0.8 convolution_multiply_fusion.4
  171.1 3.1 %reduce-scatter.2.cloned.1.call-done = bf16[128,768]{1,0:T(8,128)(2,1)} async-done(((bf16[1024,768]{1,0:T(8,128)(2,1)}), bf16[128,768]{1,0:T(8,128)(2,1)}) %reduce-scatter.2.cloned.1.call-update) | async-done | bytes 196624 | tf_op jit(solution)/shard_map/reduce_scatter | solution.py:353
  174.2 0.9 slice.37
  175.1 1.9 %collective-permute-start.1 = (bf16[64,768]{1,0:T(8,128)(2,1)S(1)}, bf16[64,768]{1,0:T(8,128)(2,1)S(1)}, u32[]{:S(2)}, u32[]{:S(2)}) collective-permute-start(bf16[64,768]{1,0:T(8,128)(2,1)S(1)} %slice.37), channel_id=1, source_target_pairs={{0,4},{4,0},{8,12},{12,8},{16,20},{20,16},{24,28},{28,24},{32,36},... | collective-permute-start | bytes 294920 | tf_op jit(solution)/shard_map/ppermute | solution.py:356
  177.1 0.6 pad_maximum_fusion.1
  177.7 2.8 %collective-permute-done.1 = bf16[64,768]{1,0:T(8,128)(2,1)S(1)} collective-permute-done((bf16[64,768]{1,0:T(8,128)(2,1)S(1)}, bf16[64,768]{1,0:T(8,128)(2,1)S(1)}, u32[]{:S(2)}, u32[]{:S(2)}) %collective-permute-start.1) | collective-permute-done | bytes 98336 | tf_op jit(solution)/shard_map/ppermute | solution.py:356
  180.5 0.9 select_bitcast_fusion.1
  181.4 0.4 multiply_convert_fusion
  181.8 0.9 copy.36
  182.7 0.9 copy.37
  (36 shorter events, 0.2 us)
Async XLA Ops:
  7.2 160.8 %copy-start = (bf16[128,7168]{1,0:T(8,128)(2,1)S(1)}, bf16[128,7168]{1,0:T(8,128)(2,1)}, u32[]{:S(2)}) copy-start(bf16[128,7168]{1,0:T(8,128)(2,1)} %param.21) | copy-start | bytes 5505028
  7.2 24.3 %copy-start.3 = (bf16[2,16,448]{2,1,0:T(8,128)(2,1)S(1)}, bf16[2,16,448]{2,1,0:T(8,128)(2,1)}, u32[]{:S(2)}) copy-start(bf16[2,16,448]{2,1,0:T(8,128)(2,1)} %own_map_ref.1) | copy-start | bytes 86020
  11.3 37.4 %all-to-all-start = ((bf16[16,8,1536]{2,1,0:T(8,128)(2,1)}), bf16[16,8,1536]{2,1,0:T(8,128)(2,1)S(1)}, u32[]{:S(2)}, u32[]{:S(2)}) async-start(bf16[16,8,1536]{2,1,0:T(8,128)(2,1)} %bitcast.80), calls=%async_computation | async-start | bytes 786432 | tf_op jit(solution)/shard_map/all_to_all | solution.py:276
  30.8 82.0 %all-gather.4.cloned.1.call-start = ((), (), s32[]{:S(2)}) async-start(), calls=%async_computation.3 | async-start | bytes 1949696 | tf_op jit(solution)/shard_map/all_gather | solution.py:251
  31.7 17.1 %copy-start.4 = (bf16[128,128]{1,0:T(8,128)(2,1)S(1)}, bf16[128,128]{1,0:T(8,128)(2,1)}, u32[]{:S(2)}) copy-start(bf16[128,128]{1,0:T(8,128)(2,1)} %get-tuple-element.27.hidden_ref) | copy-start | bytes 98308
  31.7 17.1 %copy-start.5 = (s32[1,128,8]{1,2,0:T(8,128)S(1)}, s32[1,128,8]{1,2,0:T(8,128)}, u32[]{:S(2)}) copy-start(s32[1,128,8]{1,2,0:T(8,128)} %param.14) | copy-start | bytes 12292
  31.7 17.1 %copy-start.6 = (f32[1,128,8]{1,2,0:T(8,128)S(1)}, f32[1,128,8]{1,2,0:T(8,128)}, u32[]{:S(2)}) copy-start(f32[1,128,8]{1,2,0:T(8,128)} %param.15) | copy-start | bytes 12292
  49.7 1.1 copy-start.2
  50.8 53.0 %all-to-all-start.1 = ((bf16[64,8,1408]{2,1,0:T(8,128)(2,1)}), bf16[64,8,1408]{2,1,0:T(8,128)(2,1)S(1)}, u32[]{:S(2)}, u32[]{:S(2)}) async-start(bf16[64,8,1408]{2,1,0:T(8,128)(2,1)} %bitcast.69), calls=%async_computation.1 | async-start | bytes 2883584 | tf_op jit(solution)/shard_map/all_to_all | solution.py:304
  67.6 106.6 %reduce-scatter.2.cloned.1.call-start = ((), (), s32[]{:S(2)}) async-start(), calls=%async_computation.4 | async-start | bytes 1769472 | tf_op jit(solution)/shard_map/reduce_scatter | solution.py:353
  67.7 37.5 %collective-permute-start = (bf16[448,1152]{1,0:T(8,128)(2,1)}, bf16[448,1152]{1,0:T(8,128)(2,1)}, u32[]{:S(2)}, u32[]{:S(2)}) collective-permute-start(bf16[448,1152]{1,0:T(8,128)(2,1)} %bitcast.75), channel_id=1, source_target_pairs={{0,4},{4,0},{8,12},{12,8},{16,20},{20,16},{24,28},{28,24},{32,36},... | collective-permute-start | bytes 3096584 | tf_op jit(solution)/shard_map/ppermute | solution.py:303
  105.2 1.5 copy-start.1
  112.7 26.0 %copy-start.10 = (bf16[768,448]{1,0:T(8,128)(2,1)S(1)}, bf16[768,448]{1,0:T(8,128)(2,1)}, u32[]{:S(2)}) copy-start(bf16[768,448]{1,0:T(8,128)(2,1)} %get-tuple-element.39) | copy-start | bytes 2064388
  112.8 55.1 %copy-start.7 = (bf16[1,128,7168]{2,1,0:T(8,128)(2,1)S(1)}, bf16[1,128,7168]{2,1,0:T(8,128)(2,1)}, u32[]{:S(2)}) copy-start(bf16[1,128,7168]{2,1,0:T(8,128)(2,1)} %all-gather.4.cloned.1.call-done) | copy-start | bytes 5505028
  139.0 31.1 %collective-permute-start.2 = (bf16[16,1216]{1,0:T(8,128)(2,1)S(1)}, bf16[16,1216]{1,0:T(8,128)(2,1)S(1)}, u32[]{:S(2)}, u32[]{:S(2)}) collective-permute-start(bf16[16,1216]{1,0:T(8,128)(2,1)S(1)} %pad_maximum_fusion.3), channel_id=1, source_target_pairs={{0,4},{4,0},{8,12},{12,8},{16,20},{20,16},{24,28},{28,24},{32,36},... | collective-permute-start | bytes 116744 | tf_op jit(solution)/shard_map/ppermute | solution.py:371
  167.9 0.8 copy-start.13
  167.9 0.8 copy-start.14
  167.9 0.8 copy-start.16
  167.9 2.1 %copy-start.9 = (bf16[768,448]{1,0:T(8,128)(2,1)S(1)}, bf16[768,448]{1,0:T(8,128)(2,1)}, u32[]{:S(2)}) copy-start(bf16[768,448]{1,0:T(8,128)(2,1)} %get-tuple-element.42) | copy-start | bytes 2064388
  168.0 2.4 %copy-start.8 = (bf16[64,2,768]{2,0,1:T(8,128)(2,1)S(1)}, bf16[64,2,768]{2,0,1:T(8,128)(2,1)}, u32[]{:S(2)}) copy-start(bf16[64,2,768]{2,0,1:T(8,128)(2,1)} %fusion.3) | copy-start | bytes 589828
  168.6 12.8 %copy-start.11 = (bf16[64,2,768]{2,1,0:T(2,128)(2,1)S(1)}, bf16[64,2,768]{2,1,0:T(2,128)(2,1)}, u32[]{:S(2)}) copy-start(bf16[64,2,768]{2,1,0:T(2,128)(2,1)} %param.19) | copy-start | bytes 589828
  168.6 12.8 %copy-start.12 = (bf16[64,2,768]{2,1,0:T(2,128)(2,1)S(1)}, bf16[64,2,768]{2,1,0:T(2,128)(2,1)}, u32[]{:S(2)}) copy-start(bf16[64,2,768]{2,1,0:T(2,128)(2,1)} %param.20) | copy-start | bytes 589828
  168.7 12.8 %copy-start.15 = (bf16[2,64,16]{1,2,0:T(8,128)(2,1)S(1)}, bf16[2,64,16]{1,2,0:T(8,128)(2,1)}, u32[]{:S(2)}) copy-start(bf16[2,64,16]{1,2,0:T(8,128)(2,1)} %param.17) | copy-start | bytes 12292
  175.1 5.3 %collective-permute-start.1 = (bf16[64,768]{1,0:T(8,128)(2,1)S(1)}, bf16[64,768]{1,0:T(8,128)(2,1)S(1)}, u32[]{:S(2)}, u32[]{:S(2)}) collective-permute-start(bf16[64,768]{1,0:T(8,128)(2,1)S(1)} %slice.37), channel_id=1, source_target_pairs={{0,4},{4,0},{8,12},{12,8},{16,20},{20,16},{24,28},{28,24},{32,36},... | collective-permute-start | bytes 294920 | tf_op jit(solution)/shard_map/ppermute | solution.py:356
Sparse Core Ops, SparseCore 0:
  34.3 71.2 all-gather.3
  112.9 61.3 reduce-scatter.1
